TPU v7x, 32 devices: a whole 2x2x4 slice. The times are simulated.
32 devices in a mesh: wide: 8 (over z, y), narrow: 4 (over x, core).
Axes of the slice: x: 2, y: 2, z: 4, core: 2. Of those that a mesh axis runs over, the one named last changes fastest.
Arguments:
- hidden: bfloat16 [16384, 8192], P('wide', 'narrow'), may hold values from -6 to 6
- base_key_value: bfloat16 [8192, 8, 2, 128], P('narrow'), may hold values from -0.0625 to 0.0625
- store_a: bfloat16 [64, 8192, 128], P('wide', 'narrow'), may hold values from -0.0625 to 0.0625
- stored_up_maps: bfloat16 [64, 2, 64, 8, 128], P('wide', None, None, 'narrow'), may hold values from -0.75 to 0.75
- adapter_ids: int32 [128], P('wide'), may hold values from 0 to 63, as said below
- span_start: int32 [128], P('wide'), may hold values from 0 to 31
Outputs:
- key_value: bfloat16 [8, 16384, 2, 128], P('narrow', 'wide')
Inputs may be any that keep to these rules, and one draw needn't show every extreme that they name: `adapter_ids`: requests of one replica that name different adapters name adapters of different owners, the owner of adapter a being the replica a // 8.
All inputs are finite; a program needn't handle non-finite values.
Results may differ from a plain program's by a relative error of at most 0.015.
Values may be sent and summed in bfloat16 or wider, within the bound.
A program may use at most 192 MiB of HBM per device.

v0:
```python
import jax
import jax.numpy as jnp
from jax import lax
from jax.sharding import PartitionSpec as P

THETA = 500000.0


def rotate_keys(values, positions):
    half_dim = values.shape[-1] // 2
    frequency = THETA ** (-(jnp.arange(half_dim, dtype=jnp.float32) * 2.0 / values.shape[-1]))
    angles = positions[:, None] * frequency[None, :]
    angles = jnp.concatenate([angles, angles], axis=-1)
    turned = jnp.concatenate([-values[..., half_dim:], values[..., :half_dim]], axis=-1)
    return values * jnp.cos(angles) + turned * jnp.sin(angles)


def shards(hidden, base_key_value, store_a, stored_up_maps, adapter_ids, span_start):
    wide_count = lax.axis_size("wide")
    stored = store_a.shape[0]
    requests = adapter_ids.shape[0]
    span_len = hidden.shape[0] // requests
    rank_two = store_a.shape[2]
    owners = adapter_ids // stored
    slot_ids = adapter_ids % stored
    matches = owners[None, :] == jnp.arange(wide_count, dtype=jnp.int32)[:, None]
    wanted = jnp.max(jnp.where(matches, slot_ids[None, :] + 1, 0), axis=1).reshape(wide_count, 1)
    asked_slots = lax.all_to_all(wanted, "wide", split_axis=0, concat_axis=0, tiled=True)
    filled = asked_slots[:, 0] > 0
    chosen = jnp.maximum(asked_slots[:, 0] - 1, 0)
    reply_a = jnp.where(filled[:, None, None], store_a[chosen], jnp.zeros((), jnp.bfloat16))
    reply_b = jnp.where(
        filled[:, None, None, None, None], stored_up_maps[chosen], jnp.zeros((), jnp.bfloat16)
    )
    got_a, got_b = (
        lax.all_to_all(reply_a, "wide", split_axis=0, concat_axis=0, tiled=True),
        lax.all_to_all(reply_b, "wide", split_axis=0, concat_axis=0, tiled=True),
    )
    needed_a = got_a[owners]
    needed_b = got_b[owners]
    request_rows = hidden.reshape(requests, span_len, hidden.shape[1])
    shrink_part = jnp.einsum(
        "rtd,rdc->rtc", request_rows, needed_a, preferred_element_type=jnp.float32
    )
    shrunk = lax.psum(shrink_part.astype(jnp.bfloat16), "narrow")
    base_total_sum = lax.psum_scatter(
        jnp.einsum(
            "td,dhjc->htjc", hidden, base_key_value, preferred_element_type=jnp.float32
        ).astype(jnp.bfloat16),
        "narrow",
        scatter_dimension=0,
        tiled=True,
    ).astype(jnp.float32)
    rank = rank_two // 2
    shrunk_split = shrunk.reshape(requests, span_len, 2, rank)
    delta = jnp.einsum(
        "rtjk,rjkhc->hrtjc", shrunk_split, needed_b, preferred_element_type=jnp.float32
    )
    raw = base_total_sum + delta.reshape(base_total_sum.shape)
    positions = (
        (span_start[:, None] * span_len + jnp.arange(span_len, dtype=jnp.int32)[None, :])
        .reshape(-1)
        .astype(jnp.float32)
    )
    keys_turned = jax.vmap(lambda head_keys: rotate_keys(head_keys, positions))(raw[:, :, 0, :])
    joined = jnp.stack([keys_turned, raw[:, :, 1, :]], axis=2)
    return joined.astype(jnp.bfloat16)


def solution(mesh):
    placed = (
        P("wide", "narrow"),
        P("narrow", None, None, None),
        P("wide", "narrow", None),
        P("wide", None, None, "narrow", None),
        P("wide"),
        P("wide"),
    )
    return jax.shard_map(
        shards,
        mesh=mesh,
        in_specs=placed,
        out_specs=P("narrow", "wide", None, None),
        check_vma=False,
    )
```

profile of v0, /device:TPU:8, one launch (start us, length us, event | category | flops | bytes accessed | tf_op | source)
XLA Modules:
  0.0 264.5 jit_solution(10227807450133984813)
XLA Ops:
  6.5 0.7 compare_select_fusion
  7.3 0.1 select_reduce_fusion
  7.5 11.0 %all_to_all.19 = s32[8,1,1]{2,1,0:T(1,128)S(1)} all-to-all(s32[8,1,1]{2,1,0:T(1,128)S(1)} %copy.34), channel_id=1, replica_groups=mesh['wide'=8,'narrow'=4] {'wide'}, dimensions={0} | all-to-all | bytes 64 | tf_op jit(solution)/shard_map/all_to_all | solution.py:28
  18.5 0.2 maximum_reduce_fusion
  18.8 5.2 %gather_fusion.2 = bf16[8,2048,128]{2,1,0:T(8,128)(2,1)} fusion(bf16[8,2048,128]{2,1,0:T(8,128)(2,1)} %param.8, s32[1024]{0:T(1024)S(1)} %pad_clamp_fusion.1), kind=kCustom, calls=%fused_computation.2 | custom fusion | bytes 8388640 | tf_op jit(solution)/shard_map/gather | solution.py:31
  24.0 0.2 compare_reduce_fusion
  24.2 4.5 %broadcast_select_fusion = bf16[8,2048,128]{2,1,0:T(8,128)(2,1)} fusion(bf16[8,2048,128]{2,1,0:T(8,128)(2,1)} %gather_fusion.2, pred[8]{0:T(512)(128)(4,1)S(1)} %compare_reduce_fusion), kind=kLoop, calls=%fused_computation.9 | loop fusion | flops 2097152 | bytes 8388616 | tf_op jit(solution)/shard_map/jit(_where)/select_n | solution.py:31
  28.7 6.0 %all-to-all-start.2 = ((bf16[8,2048,128]{2,1,0:T(8,128)(2,1)}), bf16[8,2048,128]{2,1,0:T(8,128)(2,1)}, u32[]{:S(2)}, u32[]{:S(2)}) async-start(bf16[8,2048,128]{2,1,0:T(8,128)(2,1)} %broadcast_select_fusion), calls=%async_computation.3 | async-start | bytes 8388608 | tf_op jit(solution)/shard_map/all_to_all | solution.py:36
  34.7 89.6 %all-to-all-done.2 = bf16[8,2048,128]{2,1,0:T(8,128)(2,1)} async-done(((bf16[8,2048,128]{2,1,0:T(8,128)(2,1)}), bf16[8,2048,128]{2,1,0:T(8,128)(2,1)}, u32[]{:S(2)}, u32[]{:S(2)}) %all-to-all-start.2) | async-done | bytes 4194336 | tf_op jit(solution)/shard_map/all_to_all | solution.py:36
  124.3 6.7 %gather_fusion.3 = bf16[16,2048,128]{2,1,0:T(8,128)(2,1)} fusion(bf16[8,2048,128]{2,1,0:T(8,128)(2,1)} %all-to-all-done.2, s32[1024]{0:T(1024)S(1)} %pad_clamp_fusion), kind=kCustom, calls=%fused_computation.3 | custom fusion | bytes 16777280 | tf_op jit(solution)/shard_map/gather | solution.py:39
  130.9 9.4 %convolution_convert_fusion = bf16[16,128,128]{2,1,0:T(8,128)(2,1)} fusion(bf16[16,2048,128]{2,1,0:T(8,128)(2,1)} %gather_fusion.3, bf16[16,128,2048]{2,1,0:T(8,128)(2,1)} %bitcast.48), kind=kOutput, calls=%fused_computation.19 | convolution fusion | flops 1074003968 | bytes 17301504 | tf_op jit(solution)/shard_map/rtd,rdc->rtc/dot_general | solution.py:42
  140.3 0.2 reduce-scatter.2.cloned.1.call-start
  140.6 25.3 %convert_bitcast_fusion = bf16[8,2048,2,128]{1,3,2,0:T(8,128)(2,1)} fusion(bf16[2048,2048]{1,0:T(8,128)(2,1)} %param.6, bf16[2048,8,2,128]{3,2,1,0:T(2,128)(2,1)} %param.7), kind=kOutput, calls=%fused_computation.7 | convolution fusion | flops 17184063488 | bytes 25165824 | tf_op jit(solution)/shard_map/td,dhjc->htjc/dot_general | solution.py:47
  165.9 0.6 copy-done.1
  166.6 1.6 gather_fusion
  168.2 1.3 broadcast_select_fusion.1
  169.5 6.2 %all-to-all-start.1 = ((bf16[8,2,64,2,128]{4,3,2,1,0:T(2,128)(2,1)}), bf16[8,2,64,2,128]{4,3,2,1,0:T(2,128)(2,1)S(1)}, u32[]{:S(2)}, u32[]{:S(2)}) async-start(bf16[8,2,64,2,128]{4,3,2,1,0:T(2,128)(2,1)} %broadcast_select_fusion.1), calls=%async_computation.2 | async-start | bytes 1048576 | tf_op jit(solution)/shard_map/all_to_all | solution.py:37
  175.7 0.1 broadcast_multiply_fusion
  175.8 3.7 %fusion.12 = (f32[2048,128]{0,1:T(8,128)S(1)}, f32[2048,128]{0,1:T(8,128)S(1)}) fusion(f32[2048,64]{0,1:T(8,128)S(1)} %broadcast_multiply_fusion), kind=kLoop, calls=%fused_computation.25 | loop fusion | flops 262144 | bytes 2621440 | tf_op jit(solution)/shard_map/vmap()/cos | solution.py:15
  179.5 9.5 %all-to-all-done.1 = bf16[8,2,64,2,128]{4,3,2,1,0:T(2,128)(2,1)S(1)} async-done(((bf16[8,2,64,2,128]{4,3,2,1,0:T(2,128)(2,1)}), bf16[8,2,64,2,128]{4,3,2,1,0:T(2,128)(2,1)S(1)}, u32[]{:S(2)}, u32[]{:S(2)}) %all-to-all-start.1) | async-done | bytes 524320 | tf_op jit(solution)/shard_map/all_to_all | solution.py:37
  189.0 3.6 %gather_fusion.1 = bf16[16,2,64,2,128]{4,3,2,1,0:T(2,128)(2,1)} fusion(bf16[8,2,64,2,128]{4,3,2,1,0:T(2,128)(2,1)S(1)} %all-to-all-done.1, s32[1024]{0:T(1024)S(1)} %pad_clamp_fusion), kind=kCustom, calls=%fused_computation.1 | custom fusion | bytes 2097216 | tf_op jit(solution)/shard_map/gather | solution.py:40
  192.6 4.2 %convolution_bitcast_fusion = f32[2,16,128,2,128]{4,2,0,3,1:T(8,128)} fusion(bf16[16,2,64,2,128]{4,3,2,1,0:T(2,128)(2,1)} %gather_fusion.1, bf16[16,128,2,64]{1,3,2,0:T(8,128)(2,1)} %all-reduce.2.cloned.1.call-done), kind=kOutput, calls=%fused_computation.10 | convolution fusion | flops 134217728 | bytes 5767168 | tf_op jit(solution)/shard_map/rtjk,rjkhc->hrtjc/dot_general | solution.py:56
  196.8 5.5 %copy.37 = f32[2,16,128,2,128]{2,1,4,3,0:T(8,128)} copy(f32[2,16,128,2,128]{4,2,0,3,1:T(8,128)} %convolution_bitcast_fusion) | data formatting | bytes 8388608 | tf_op jit(solution)/shard_map/rtjk,rjkhc->hrtjc/transpose | solution.py:56
  202.3 4.9 %reshape.149 = f32[2,2048,2,128]{1,3,2,0:T(8,128)} reshape(f32[2,16,128,2,128]{2,1,4,3,0:T(8,128)} %copy.37) | data formatting | bytes 8388608 | tf_op jit(solution)/shard_map/reshape | solution.py:59
  207.1 41.9 %reduce-scatter.2.cloned.1.call-done = bf16[2,2048,2,128]{1,3,2,0:T(8,128)(2,1)} async-done(((bf16[8,2048,2,128]{1,3,2,0:T(8,128)(2,1)}), bf16[2,2048,2,128]{1,3,2,0:T(8,128)(2,1)}) %reduce-scatter.2.cloned.1.call-update) | async-done | bytes 2097168 | tf_op jit(solution)/shard_map/reduce_scatter | solution.py:46
  249.0 3.5 %convert_add_fusion = f32[2,2048,2,128]{1,3,2,0:T(8,128)S(1)} fusion(f32[2,2048,2,128]{1,3,2,0:T(8,128)} %reshape.149, bf16[2,2048,2,128]{1,3,2,0:T(8,128)(2,1)} %reduce-scatter.2.cloned.1.call-done), kind=kLoop, calls=%fused_computation.8 | loop fusion | flops 2097152 | bytes 10485760 | tf_op jit(solution)/shard_map/add | solution.py:59
  252.5 0.1 slice_bitcast_fusion
  252.7 0.1 slice.36
  252.8 0.1 fusion.10
  253.0 0.7 fusion.8
  253.6 0.2 pad_maximum_fusion
  253.8 3.8 %copy.41 = bf16[2,2048,2,128]{3,2,1,0:T(2,128)(2,1)} copy(bf16[2,2048,2,128]{1,3,2,0:T(8,128)(2,1)S(1)} %pad_maximum_fusion) | data formatting | bytes 4194304 | tf_op jit(solution)/shard_map/stack | solution.py:66
  (13 shorter events, 0.2 us)
Async XLA Ops:
  6.5 160.0 %copy-start = (bf16[8,2,64,2,128]{4,3,2,1,0:T(2,128)(2,1)S(1)}, bf16[8,2,64,2,128]{4,3,2,1,0:T(2,128)(2,1)}, u32[]{:S(2)}) copy-start(bf16[8,2,64,2,128]{4,3,2,1,0:T(2,128)(2,1)} %param.9) | copy-start | bytes 1572868
  28.7 95.6 %all-to-all-start.2 = ((bf16[8,2048,128]{2,1,0:T(8,128)(2,1)}), bf16[8,2048,128]{2,1,0:T(8,128)(2,1)}, u32[]{:S(2)}, u32[]{:S(2)}) async-start(bf16[8,2048,128]{2,1,0:T(8,128)(2,1)} %broadcast_select_fusion), calls=%async_computation.3 | async-start | bytes 8388608 | tf_op jit(solution)/shard_map/all_to_all | solution.py:36
  34.7 157.9 %all-reduce.2.cloned.1.call-start = ((), (), s32[]{:S(2)}) async-start(), calls=%async_computation.5 | async-start | bytes 1048576 | tf_op jit(solution)/shard_map/psum | solution.py:45
  140.3 108.7 %reduce-scatter.2.cloned.1.call-start = ((), (), s32[]{:S(2)}) async-start(), calls=%async_computation.4 | async-start | bytes 10485760 | tf_op jit(solution)/shard_map/reduce_scatter | solution.py:46
  165.9 0.7 copy-start.1
  169.5 19.6 %all-to-all-start.1 = ((bf16[8,2,64,2,128]{4,3,2,1,0:T(2,128)(2,1)}), bf16[8,2,64,2,128]{4,3,2,1,0:T(2,128)(2,1)S(1)}, u32[]{:S(2)}, u32[]{:S(2)}) async-start(bf16[8,2,64,2,128]{4,3,2,1,0:T(2,128)(2,1)} %broadcast_select_fusion.1), calls=%async_computation.2 | async-start | bytes 1048576 | tf_op jit(solution)/shard_map/all_to_all | solution.py:37
Sparse Core Ops, SparseCore 0:
  140.5 34.2 all-reduce.1
  177.3 71.7 reduce-scatter.1
where the time goes:
time: 267 us; the launch traced here: 264 us
  waiting for transfers between devices  141 us (53%)
  matrix products  38.9 us (15%)
  local copies, waits for them, and re-layouts  32.2 us (12%)
  other arithmetic  15.5 us (6%)
  between operations  13.5 us (5%)
  starting transfers between devices  12.4 us (5%)
  blocking collectives  11 us (4%)
    all_to_all x1, waiting for transfers between devices, shards(): lax.all_to_all(reply_a, 'wide', split_axis=0, concat_axis=0, tiled=True)  89.6 us
    reduce_scatter x1, waiting for transfers between devices, shards(): lax.psum_scatter(jnp.einsum('td,dhjc->htjc', hidden, base_key_value, pref...  41.9 us
    dot_general x1, matrix products, shards(): jnp.einsum('td,dhjc->htjc', hidden, base_key_value, preferred_element_typ...  25.3 us
    all_to_all x1, blocking collectives, shards(): lax.all_to_all(wanted, 'wide', split_axis=0, concat_axis=0, tiled=True)  11 us
    all_to_all x1, waiting for transfers between devices, shards(): lax.all_to_all(reply_b, 'wide', split_axis=0, concat_axis=0, tiled=True)  9.52 us
    dot_general x1, matrix products, shards(): jnp.einsum('rtd,rdc->rtc', request_rows, needed_a, preferred_element_type...  9.4 us
    gather x1, local copies, waits for them, and re-layouts, shards(): needed_a = got_a[owners]  6.66 us
    all_to_all x1, starting transfers between devices, shards(): lax.all_to_all(reply_b, 'wide', split_axis=0, concat_axis=0, tiled=True)  6.17 us
  transfers between devices with their start and end apart: 4, of which 3 were waited for; matrix products, arithmetic and copies ran while one was open for 19% of the time, Pallas kernels for 0%

commit v1 on v0

v1 whole, which is shorter than its diff:
```python
import functools

import jax
import jax.numpy as jnp
from jax import lax
from jax.experimental import pallas as pl
from jax.experimental.pallas import tpu as pltpu
from jax.sharding import PartitionSpec as P

THETA = 500000.0
MESH = pl.DeviceIdType.MESH
F32, BF16 = jnp.float32, jnp.bfloat16


def flip(index, k, bits):
    total = 0
    for b in range(bits):
        bit = lax.rem(index // (1 << b), 2)
        total = total + lax.rem(bit + ((k >> b) & 1), 2) * (1 << b)
    return total


def pick(chosen, a_ref, b_ref, ra_ref, rb_ref):
    ra_ref[...] = a_ref[...]
    rb_ref[...] = b_ref[...]


def main(
    nw, nx, slot_ref, hid_hbm, w_hbm, ra, rb, ca, sa, cb, sb, out,
    hid, w, abuf, bbuf, psend, prec, xsend, xrec, base, acc, s1s, s1r, s2s, s2r, finm, fino,
    lsem, wsem, a_s, a_r, b_s, b_r, p_s, p_r, x_s, x_r, t_s, t_r,
):
    bits = nw.bit_length() - 1
    wi, ni = lax.axis_index("wide"), lax.axis_index("narrow")
    xi, ci = ni // 2, lax.rem(ni, 2)
    tokens, cols = base.shape
    half = tokens // 2
    span = cb.shape[0]
    heads = cols // 256
    partner = (wi, xi * 2 + 1 - ci)
    across = [(wi, lax.rem(xi + d, nx) * 2 + ci) for d in range(1, nx)]
    replicas = [(flip(wi, k, bits), ni) for k in range(1, nw)]

    barrier = pltpu.get_barrier_semaphore()
    for peer in [partner, *across, *replicas]:
        pl.semaphore_signal(barrier, inc=1, device_id=peer, device_id_type=MESH)

    hid_copy = pltpu.make_async_copy(hid_hbm, hid, lsem.at[0])
    hid_copy.start()
    order = [(d, 1) for d in [*range(1, nx), 0]] + [(d, 0) for d in [*range(1, nx), 0]]
    w_copies = []
    for i, (d, other) in enumerate(order):
        core = 1 - ci if other else ci
        block = lax.rem(xi + d, nx) * 2 + core
        w_copies.append(pltpu.make_async_copy(w_hbm.at[block], w.at[i], wsem.at[i]))
        w_copies[-1].start()
    own_a = pltpu.make_async_copy(ra.at[wi], abuf.at[0], lsem.at[1])
    own_b = pltpu.make_async_copy(rb.at[wi], bbuf.at[0], lsem.at[2])
    own_a.start()
    own_b.start()

    pl.semaphore_wait(barrier, nw - 1 + nx)

    def remote(src, dst, s, r, peer):
        return pltpu.make_async_remote_copy(
            src_ref=src, dst_ref=dst, send_sem=s, recv_sem=r, device_id=peer, device_id_type=MESH
        )

    a_copies, b_copies = {}, {}
    for k in [*range(nw // 2, nw), *range(1, nw // 2)]:
        to = replicas[k - 1]
        a_copies[k] = remote(ra.at[to[0]], abuf.at[k], a_s.at[k], a_r.at[k], to)
        b_copies[k] = remote(rb.at[to[0]], bbuf.at[k], b_s.at[k], b_r.at[k], to)
        b_copies[k].start()
        a_copies[k].start()

    tile = 512
    hid_copy.wait()

    def product(i, store):
        w_copies[i].wait()

        def body(t, carry):
            rows = pl.ds(pl.multiple_of(t * tile, tile), tile)
            store(rows, jnp.dot(hid[rows, :], w[i], preferred_element_type=F32))
            return carry

        lax.fori_loop(0, tokens // tile, body, 0)

    p_copies, x_copies = {}, {}
    for i, (d, other) in enumerate(order):
        if other:

            def to_partner(rows, value, d=d):
                psend[d, rows, :] = value.astype(BF16)

            product(i, to_partner)
            p_copies[d] = remote(psend.at[d], prec.at[d], p_s.at[d], p_r.at[d], partner)
            p_copies[d].start()
        elif d:

            def to_across(rows, value, d=d):
                xsend[d - 1, rows, :] = (value + prec[d, rows, :].astype(F32)).astype(BF16)

            p_copies[d].wait()
            product(i, to_across)
            x_copies[d] = remote(xsend.at[d - 1], xrec.at[d - 1], x_s.at[d], x_r.at[d], across[d - 1])
            x_copies[d].start()
        else:

            def to_base(rows, value):
                base[rows, :] = value + prec[0, rows, :].astype(F32)

            p_copies[0].wait()
            product(i, to_base)

    for k in range(0, nw, 2):
        if k:
            a_copies[k].wait()
            a_copies[k + 1].wait()
        else:
            own_a.wait()
            a_copies[1].wait()

        def shrink(t, carry, k=k):
            both = jnp.concatenate([abuf[k], abuf[k + 1]], axis=1)
            rows = pl.ds(pl.multiple_of(t * tile, tile), tile)
            made = jnp.dot(hid[rows, :], both, preferred_element_type=F32)
            for q in range(tile // span):
                slot = slot_ref[t * (tile // span) + q]
                part = pl.ds(pl.multiple_of(t * tile + q * span, span), span)
                mine = made[q * span : (q + 1) * span]
                before = acc[part, :] if k else jnp.zeros((span, 128), F32)
                acc[part, :] = jnp.where(
                    slot == k, mine[:, :128], jnp.where(slot == k + 1, mine[:, 128:], before)
                )
            return carry

        lax.fori_loop(0, tokens // tile, shrink, 0)

    mine0 = pl.multiple_of(ci * half, half)
    other0 = pl.multiple_of((1 - ci) * half, half)
    s1s[...] = acc[pl.ds(other0, half), :].astype(BF16)
    first = remote(s1s, s1r, t_s.at[0], t_r.at[0], partner)
    first.start()
    for d in range(1, nx):
        x_copies[d].wait()
    own_b.wait()
    for k in range(1, nw):
        b_copies[k].wait()
    first.wait()
    summed = acc[pl.ds(mine0, half), :] + s1r[...].astype(F32)
    acc[pl.ds(mine0, half), :] = summed
    s2s[...] = summed.astype(BF16)
    seconds = []
    for d in range(1, nx):
        seconds.append(remote(s2s, s2r.at[d - 1], t_s.at[d], t_r.at[d], across[d - 1]))
        seconds[-1].start()
    for copy in seconds:
        copy.wait()
    total = acc[pl.ds(mine0, half), :]
    for d in range(1, nx):
        total = total + s2r[d - 1].astype(F32)
    finm[...] = total.astype(BF16)
    last = remote(finm, fino, t_s.at[nx], t_r.at[nx], partner)
    last.start()

    def finish(source, row0):
        def body(q, carry):
            rows = pl.ds(pl.multiple_of(row0 + q * span, span), span)
            r = row0 // span + q
            b = bbuf[slot_ref[r]]
            upper = lax.broadcasted_iota(jnp.int32, b.shape, 0) < b.shape[0] // 2
            zero = jnp.zeros_like(b)
            maps = jnp.concatenate([jnp.where(upper, b, zero), jnp.where(upper, zero, b)], axis=1)
            low = source[pl.ds(pl.multiple_of(q * span, span), span), :]
            delta = jnp.dot(low, maps, preferred_element_type=F32)
            raw = base[rows, :]
            for d in range(1, nx):
                raw = raw + xrec[d - 1, rows, :].astype(F32)
            cos_a, sin_a = ca[pl.ds(r, 1), :], sa[pl.ds(r, 1), :]
            cos = cos_a * cb[...] - sin_a * sb[...]
            sin = sin_a * cb[...] + cos_a * sb[...]
            lane = lax.broadcasted_iota(jnp.int32, sin.shape, 1)
            sin = jnp.where(lane < 64, -sin, sin)
            for h in range(heads):
                key = raw[:, h * 256 : h * 256 + 128] + delta[:, h * 128 : (h + 1) * 128]
                value = raw[:, h * 256 + 128 : (h + 1) * 256]
                value = value + delta[:, (heads + h) * 128 : (heads + h + 1) * 128]
                out[h, 0, rows, :] = (key * cos + pltpu.roll(key, 64, 1) * sin).astype(BF16)
                out[h, 1, rows, :] = value.astype(BF16)
            return carry

        lax.fori_loop(0, half // span, body, 0)

    finish(finm, mine0)
    last.wait()
    finish(fino, other0)


def shards(hidden, base_key_value, store_a, stored_up_maps, adapter_ids, span_start):
    nw, nn = lax.axis_size("wide"), lax.axis_size("narrow")
    nx = nn // 2
    stored, features, rank_two = store_a.shape
    requests = adapter_ids.shape[0]
    tokens = hidden.shape[0]
    span = tokens // requests
    cols = base_key_value.shape[1] * 256 // nn
    owners = adapter_ids // stored
    slot_ids = adapter_ids % stored
    matches = owners[None, :] == jnp.arange(nw, dtype=jnp.int32)[:, None]
    wanted = jnp.max(jnp.where(matches, slot_ids[None, :] + 1, 0), axis=1).reshape(nw, 1)
    asked = lax.all_to_all(wanted, "wide", split_axis=0, concat_axis=0, tiled=True)
    chosen = jnp.maximum(asked[:, 0] - 1, 0)
    arrival = owners ^ lax.axis_index("wide").astype(jnp.int32)

    up = stored_up_maps.reshape(stored, rank_two, -1)
    across = up.shape[2]
    ra, rb = pl.pallas_call(
        pick,
        grid_spec=pltpu.PrefetchScalarGridSpec(
            num_scalar_prefetch=1,
            grid=(nw,),
            in_specs=[
                pl.BlockSpec((1, features, rank_two), lambda i, c: (c[i], 0, 0)),
                pl.BlockSpec((1, rank_two, across), lambda i, c: (c[i], 0, 0)),
            ],
            out_specs=[
                pl.BlockSpec((1, features, rank_two), lambda i, c: (i, 0, 0)),
                pl.BlockSpec((1, rank_two, across), lambda i, c: (i, 0, 0)),
            ],
        ),
        out_shape=[
            jax.ShapeDtypeStruct((nw, features, rank_two), BF16),
            jax.ShapeDtypeStruct((nw, rank_two, across), BF16),
        ],
    )(chosen, store_a, up)

    weights = base_key_value.reshape(features, nn, cols).transpose(1, 0, 2)
    frequency = THETA ** (-(jnp.arange(64, dtype=F32) * 2.0 / 128))
    frequency = jnp.concatenate([frequency, frequency])[None, :]
    start = (span_start * span).astype(F32)[:, None] * frequency
    step = jnp.arange(span, dtype=F32)[:, None] * frequency

    vmem, smem, hbm = (pl.BlockSpec(memory_space=m) for m in (pltpu.VMEM, pltpu.SMEM, pl.ANY))
    dma = pltpu.SemaphoreType.DMA
    half = tokens // 2
    heads = cols // 256
    out = pl.pallas_call(
        functools.partial(main, nw, nx),
        out_shape=jax.ShapeDtypeStruct((heads, 2, tokens, 128), BF16),
        in_specs=[smem, hbm, hbm, hbm, hbm, vmem, vmem, vmem, vmem],
        out_specs=vmem,
        scratch_shapes=[
            pltpu.VMEM((tokens, features), BF16),
            pltpu.VMEM((nn, features, cols), BF16),
            pltpu.VMEM((nw, features, rank_two), BF16),
            pltpu.VMEM((nw, rank_two, across), BF16),
            pltpu.VMEM((nx, tokens, cols), BF16),
            pltpu.VMEM((nx, tokens, cols), BF16),
            pltpu.VMEM((nx - 1, tokens, cols), BF16),
            pltpu.VMEM((nx - 1, tokens, cols), BF16),
            pltpu.VMEM((tokens, cols), F32),
            pltpu.VMEM((tokens, rank_two), F32),
            pltpu.VMEM((half, rank_two), BF16),
            pltpu.VMEM((half, rank_two), BF16),
            pltpu.VMEM((half, rank_two), BF16),
            pltpu.VMEM((nx - 1, half, rank_two), BF16),
            pltpu.VMEM((half, rank_two), BF16),
            pltpu.VMEM((half, rank_two), BF16),
            dma((3,)), dma((nn,)), dma((nw,)), dma((nw,)), dma((nw,)), dma((nw,)),
            dma((nx,)), dma((nx,)), dma((nx,)), dma((nx,)), dma((nx + 1,)), dma((nx + 1,)),
        ],
        compiler_params=pltpu.CompilerParams(
            collective_id=0, has_side_effects=True, vmem_limit_bytes=58 * 2**20
        ),
        cost_estimate=pl.CostEstimate(
            flops=2 * tokens * features * 3072, bytes_accessed=2**25, transcendentals=0
        ),
    )(arrival, hidden, weights, ra, rb, jnp.cos(start), jnp.sin(start), jnp.cos(step), jnp.sin(step))
    return out.transpose(0, 2, 1, 3)


def solution(mesh):
    placed = (
        P("wide", "narrow"),
        P("narrow", None, None, None),
        P("wide", "narrow", None),
        P("wide", None, None, "narrow", None),
        P("wide"),
        P("wide"),
    )
    return jax.shard_map(
        shards,
        mesh=mesh,
        in_specs=placed,
        out_specs=P("narrow", "wide", None, None),
        check_vma=False,
    )
```

time: 267 us -> 184 us (0.69)
  waiting for transfers between devices: 141 us -> 0.01 us
  Pallas kernels: 0 us -> 132 us
  matrix products: 38.9 us -> 0 us
  between operations: 13.5 us -> 0.02 us
  other arithmetic: 15.5 us -> 3.85 us
  blocking collectives: 11 us -> 0 us
  local copies, waits for them, and re-layouts: 32.2 us -> 40.4 us
  starting transfers between devices: 12.4 us -> 6.28 us
    pallas_call x0 -> x2, Pallas kernels: none -> 132 us  [the longest x1 124 us: shards(): pl.pallas_call(functools.partial(main, nw, nx), out_shape=jax.ShapeDtypeS...]
    all_to_all x2 -> x1, waiting for transfers between devices: 99.1 us -> 0.01 us  [shards(): lax.all_to_all(wanted, 'wide', split_axis=0, concat_axis=0, tiled=True)]
    reduce_scatter x1 -> x0, waiting for transfers between devices: 41.9 us -> none  [shards(): lax.psum_scatter(jnp.einsum('td,dhjc->htjc', hidden, base_key_value, pref...]
    dot_general x3 -> x0, matrix products: 38.9 us -> none  [the longest x1 25.3 us: shards(): jnp.einsum('td,dhjc->htjc', hidden, base_key_value, preferred_element_typ...]
    unnamed x4 -> x5, local copies, waits for them, and re-layouts: 0.62 us -> 21.1 us
    gather x4 -> x0, local copies, waits for them, and re-layouts: 17 us -> none  [the longest x1 6.66 us: shards(): needed_a = got_a[owners]]
    all_to_all x1 -> x0, blocking collectives: 11 us -> none  [shards(): lax.all_to_all(wanted, 'wide', split_axis=0, concat_axis=0, tiled=True)]
    reshape x1 -> x2, local copies, waits for them, and re-layouts: 4.89 us -> 12.6 us  [the longest x1 11.5 us: shards(): weights = base_key_value.reshape(features, nn, cols).transpose(1, 0, 2)]
  transfers between devices with their start and end apart: 4 -> 1, of which waited for: 3 -> 0; matrix products, arithmetic and copies ran while one was open for 19% -> 19% of each run, Pallas kernels for 0% -> 0%
where the time goes in v1:
time: 184 us; the launch traced here: 183 us
  Pallas kernels  132 us (72%)
  local copies, waits for them, and re-layouts  40.4 us (22%)
  starting transfers between devices  6.28 us (3%)
  other arithmetic  3.85 us (2%)
    pallas_call x1, Pallas kernels, shards(): pl.pallas_call(functools.partial(main, nw, nx), out_shape=jax.ShapeDtypeS...  124 us
    unnamed x5, local copies, waits for them, and re-layouts  21.1 us
    reshape x1, local copies, waits for them, and re-layouts, shards(): weights = base_key_value.reshape(features, nn, cols).transpose(1, 0, 2)  11.5 us
    pallas_call x1, Pallas kernels, shards(): pl.pallas_call(pick, grid_spec=pltpu.PrefetchScalarGridSpec(num_scalar_pr...  7.6 us
    all_to_all x1, starting transfers between devices, shards(): lax.all_to_all(wanted, 'wide', split_axis=0, concat_axis=0, tiled=True)  6.28 us
    transpose x1, local copies, waits for them, and re-layouts, shards(): return out.transpose(0, 2, 1, 3)  5.99 us
  transfers between devices with their start and end apart: 1, of which 0 were waited for; matrix products, arithmetic and copies ran while one was open for 19% of the time, Pallas kernels for 0%

profile of v1, /device:TPU:8, one launch (start us, length us, event | category | flops | bytes accessed | tf_op | source)
XLA Modules:
  0.0 182.6 jit_solution(15746068802231841027)
XLA Ops:
  0.0 1.2 broadcast_xor_fusion
  1.2 0.1 select_reduce_fusion
  1.3 0.7 copy.21
  2.0 6.3 %all-to-all-start = ((s32[8,1,1]{2,1,0:T(1,128)}), s32[8,1,1]{2,1,0:T(1,128)S(1)}, u32[]{:S(2)}, u32[]{:S(2)}) async-start(s32[8,1,1]{2,1,0:T(1,128)} %copy.21), calls=%async_computation | async-start | bytes 8192 | tf_op jit(solution)/shard_map/all_to_all | solution.py:213
  8.3 21.1 %copy.19 = bf16[2048,8,2,128]{0,3,2,1:T(8,128)(2,1)} copy(bf16[2048,8,2,128]{3,2,1,0:T(2,128)(2,1)} %param.7) | data formatting | bytes 16777216 | tf_op args[1]
  29.4 0.0 copy-start.1
  29.4 0.0 copy-start
  29.4 11.5 %copy.20 = bf16[2048,4,512]{2,0,1:T(8,128)(2,1)} copy(bf16[2048,4,512]{0,2,1:T(8,128)(2,1)} %bitcast.4) | data formatting | bytes 16777216 | tf_op jit(solution)/shard_map/reshape | solution.py:239
  40.9 0.1 pad_maximum_fusion
  40.9 0.0 copy-done.1
  41.0 0.9 fusion
  41.9 0.7 multiply_sine_fusion
  42.6 0.0 copy-done
  42.6 1.1 reshape.21.b_ref
  43.7 0.0 all-to-all-done
  43.7 0.8 maximum_reduce_fusion.chosen
  44.5 7.6 %shard_map.64 = (bf16[8,2048,128]{2,1,0:T(8,128)(2,1)}, bf16[8,128,256]{2,1,0:T(8,128)(2,1)}) custom-call(s32[8]{0:T(128)} %maximum_reduce_fusion.chosen, bf16[8,2048,128]{2,1,0:T(8,128)(2,1)} %a_ref.1, bf16[8,128,256]{2,1,0:T(8,128)(2,1)} %reshape.21.b_ref), custom_call_target="tpu_custom_call" | custom-call | tf_op jit(solution)/shard_map/pallas_call | solution.py:219
  52.1 124.5 %shard_map.65 = bf16[2,2,2048,128]{3,2,1,0:T(8,128)(2,1)} custom-call(s32[16]{0:T(128)} %get-tuple-element.9.slot_ref, bf16[2048,2048]{1,0:T(8,128)(2,1)} %hid_hbm.1, bf16[4,2048,512]{2,1,0:T(8,128)(2,1)} %bitcast.5, bf16[8,2048,128]{2,1,0:T(8,128)(2,1)} %get-tuple-element.7.ra, bf16[8,128,256]{2,1,0:T(8,128)(2,1)} %get-tuple-element.8.rb, ...), custom_call_target="tpu_custom_call" | custom-call | flops 25769803776 | bytes 33554432 | tf_op jit(solution)/shard_map/pallas_call | solution.py:249
  176.6 6.0 %copy.22 = bf16[2,2048,2,128]{3,2,1,0:T(2,128)(2,1)} copy(bf16[2,2048,2,128]{3,1,2,0:T(8,128)(2,1)} %bitcast.6) | data formatting | bytes 4194304 | tf_op jit(solution)/shard_map/transpose | solution.py:281
  (2 shorter events, 0.0 us)
Async XLA Ops:
  2.0 41.7 %all-to-all-start = ((s32[8,1,1]{2,1,0:T(1,128)}), s32[8,1,1]{2,1,0:T(1,128)S(1)}, u32[]{:S(2)}, u32[]{:S(2)}) async-start(s32[8,1,1]{2,1,0:T(1,128)} %copy.21), calls=%async_computation | async-start | bytes 8192 | tf_op jit(solution)/shard_map/all_to_all | solution.py:213
  29.4 11.6 %copy-start.1 = (s32[16]{0:T(128)S(1)}, s32[16]{0:T(128)}, u32[]{:S(2)}) copy-start(s32[16]{0:T(128)} %param.11) | copy-start | bytes 196
  29.4 13.2 %copy-start = (bf16[8,2,64,2,128]{4,3,2,1,0:T(2,128)(2,1)S(1)}, bf16[8,2,64,2,128]{4,3,2,1,0:T(2,128)(2,1)}, u32[]{:S(2)}) copy-start(bf16[8,2,64,2,128]{4,3,2,1,0:T(2,128)(2,1)} %param.9) | copy-start | bytes 1572868

commit v2 on v1

--- a/solution.py
+++ b/solution.py
@@ -20,15 +20,10 @@
     return total
 
 
-def pick(chosen, a_ref, b_ref, ra_ref, rb_ref):
-    ra_ref[...] = a_ref[...]
-    rb_ref[...] = b_ref[...]
-
-
 def main(
-    nw, nx, slot_ref, hid_hbm, w_hbm, ra, rb, ca, sa, cb, sb, out,
-    hid, w, abuf, bbuf, psend, prec, xsend, xrec, base, acc, s1s, s1r, s2s, s2r, finm, fino,
-    lsem, wsem, a_s, a_r, b_s, b_r, p_s, p_r, x_s, x_r, t_s, t_r,
+    nw, nx, slot_ref, chosen_ref, hid_hbm, w_hbm, store_hbm, up, ca, sa, cb, sb, out,
+    hid, raw_w, w, store, ra, rb, abuf, bbuf, psend, prec, xsend, xrec, base, acc, s1s, s1r, s2s, s2r, finm, fino,
+    lsem, a_s, a_r, b_s, b_r, p_s, p_r, x_s, x_r, t_s, t_r,
 ):
     bits = nw.bit_length() - 1
     wi, ni = lax.axis_index("wide"), lax.axis_index("narrow")
@@ -45,19 +40,14 @@
     for peer in [partner, *across, *replicas]:
         pl.semaphore_signal(barrier, inc=1, device_id=peer, device_id_type=MESH)
 
-    hid_copy = pltpu.make_async_copy(hid_hbm, hid, lsem.at[0])
+    store_copy = pltpu.make_async_copy(store_hbm, store, lsem.at[0])
+    store_copy.start()
+    w_copy = pltpu.make_async_copy(w_hbm, raw_w, lsem.at[1])
+    w_copy.start()
+    hid_copy = pltpu.make_async_copy(hid_hbm, hid, lsem.at[2])
     hid_copy.start()
     order = [(d, 1) for d in [*range(1, nx), 0]] + [(d, 0) for d in [*range(1, nx), 0]]
-    w_copies = []
-    for i, (d, other) in enumerate(order):
-        core = 1 - ci if other else ci
-        block = lax.rem(xi + d, nx) * 2 + core
-        w_copies.append(pltpu.make_async_copy(w_hbm.at[block], w.at[i], wsem.at[i]))
-        w_copies[-1].start()
-    own_a = pltpu.make_async_copy(ra.at[wi], abuf.at[0], lsem.at[1])
-    own_b = pltpu.make_async_copy(rb.at[wi], bbuf.at[0], lsem.at[2])
-    own_a.start()
-    own_b.start()
+    store_copy.wait()
 
     pl.semaphore_wait(barrier, nw - 1 + nx)
 
@@ -69,20 +59,37 @@
     a_copies, b_copies = {}, {}
     for k in [*range(nw // 2, nw), *range(1, nw // 2)]:
         to = replicas[k - 1]
-        a_copies[k] = remote(ra.at[to[0]], abuf.at[k], a_s.at[k], a_r.at[k], to)
-        b_copies[k] = remote(rb.at[to[0]], bbuf.at[k], b_s.at[k], b_r.at[k], to)
+        ra[k] = store[chosen_ref[to[0]]]
+        rb[k] = up[chosen_ref[to[0]]]
+        a_copies[k] = remote(ra.at[k], abuf.at[k], a_s.at[k], a_r.at[k], to)
+        b_copies[k] = remote(rb.at[k], bbuf.at[k], b_s.at[k], b_r.at[k], to)
         b_copies[k].start()
         a_copies[k].start()
 
+    abuf[0] = store[chosen_ref[wi]]
+    bbuf[0] = up[chosen_ref[wi]]
     tile = 512
+    w_copy.wait()
     hid_copy.wait()
 
     def product(i, store):
-        w_copies[i].wait()
+        d, other = order[i]
+        block = lax.rem(xi + d, nx) * 2 + (1 - ci if other else ci)
+        step = 256
+
+        def unpack(t, carry):
+            rows = pl.ds(pl.multiple_of(t * step, step), step)
+            for h in range(heads):
+                pair = raw_w[rows, block * heads + h].astype(F32)
+                for j in range(2):
+                    w[rows, (2 * h + j) * 128 : (2 * h + j + 1) * 128] = pair[:, j, :].astype(BF16)
+            return carry
+
+        lax.fori_loop(0, w.shape[0] // step, unpack, 0)
 
         def body(t, carry):
             rows = pl.ds(pl.multiple_of(t * tile, tile), tile)
-            store(rows, jnp.dot(hid[rows, :], w[i], preferred_element_type=F32))
+            store(rows, jnp.dot(hid[rows, :], w[...], preferred_element_type=F32))
             return carry
 
         lax.fori_loop(0, tokens // tile, body, 0)
@@ -119,7 +126,6 @@
             a_copies[k].wait()
             a_copies[k + 1].wait()
         else:
-            own_a.wait()
             a_copies[1].wait()
 
         def shrink(t, carry, k=k):
@@ -145,7 +151,6 @@
     first.start()
     for d in range(1, nx):
         x_copies[d].wait()
-    own_b.wait()
     for k in range(1, nw):
         b_copies[k].wait()
     first.wait()
@@ -216,27 +221,6 @@
 
     up = stored_up_maps.reshape(stored, rank_two, -1)
     across = up.shape[2]
-    ra, rb = pl.pallas_call(
-        pick,
-        grid_spec=pltpu.PrefetchScalarGridSpec(
-            num_scalar_prefetch=1,
-            grid=(nw,),
-            in_specs=[
-                pl.BlockSpec((1, features, rank_two), lambda i, c: (c[i], 0, 0)),
-                pl.BlockSpec((1, rank_two, across), lambda i, c: (c[i], 0, 0)),
-            ],
-            out_specs=[
-                pl.BlockSpec((1, features, rank_two), lambda i, c: (i, 0, 0)),
-                pl.BlockSpec((1, rank_two, across), lambda i, c: (i, 0, 0)),
-            ],
-        ),
-        out_shape=[
-            jax.ShapeDtypeStruct((nw, features, rank_two), BF16),
-            jax.ShapeDtypeStruct((nw, rank_two, across), BF16),
-        ],
-    )(chosen, store_a, up)
-
-    weights = base_key_value.reshape(features, nn, cols).transpose(1, 0, 2)
     frequency = THETA ** (-(jnp.arange(64, dtype=F32) * 2.0 / 128))
     frequency = jnp.concatenate([frequency, frequency])[None, :]
     start = (span_start * span).astype(F32)[:, None] * frequency
@@ -249,11 +233,15 @@
     out = pl.pallas_call(
         functools.partial(main, nw, nx),
         out_shape=jax.ShapeDtypeStruct((heads, 2, tokens, 128), BF16),
-        in_specs=[smem, hbm, hbm, hbm, hbm, vmem, vmem, vmem, vmem],
+        in_specs=[smem, smem, hbm, hbm, hbm, vmem, vmem, vmem, vmem, vmem],
         out_specs=vmem,
         scratch_shapes=[
             pltpu.VMEM((tokens, features), BF16),
-            pltpu.VMEM((nn, features, cols), BF16),
+            pltpu.VMEM(base_key_value.shape, BF16),
+            pltpu.VMEM((features, cols), BF16),
+            pltpu.VMEM(store_a.shape, BF16),
+            pltpu.VMEM((nw, features, rank_two), BF16),
+            pltpu.VMEM((nw, rank_two, across), BF16),
             pltpu.VMEM((nw, features, rank_two), BF16),
             pltpu.VMEM((nw, rank_two, across), BF16),
             pltpu.VMEM((nx, tokens, cols), BF16),
@@ -268,7 +256,7 @@
             pltpu.VMEM((nx - 1, half, rank_two), BF16),
             pltpu.VMEM((half, rank_two), BF16),
             pltpu.VMEM((half, rank_two), BF16),
-            dma((3,)), dma((nn,)), dma((nw,)), dma((nw,)), dma((nw,)), dma((nw,)),
+            dma((3,)), dma((nw,)), dma((nw,)), dma((nw,)), dma((nw,)),
             dma((nx,)), dma((nx,)), dma((nx,)), dma((nx,)), dma((nx + 1,)), dma((nx + 1,)),
         ],
         compiler_params=pltpu.CompilerParams(
@@ -277,7 +265,7 @@
         cost_estimate=pl.CostEstimate(
             flops=2 * tokens * features * 3072, bytes_accessed=2**25, transcendentals=0
         ),
-    )(arrival, hidden, weights, ra, rb, jnp.cos(start), jnp.sin(start), jnp.cos(step), jnp.sin(step))
+    )(arrival, chosen, hidden, base_key_value, store_a, up, jnp.cos(start), jnp.sin(start), jnp.cos(step), jnp.sin(step))
     return out.transpose(0, 2, 1, 3)
 
 

time: 184 us -> 145 us (0.79)
  local copies, waits for them, and re-layouts: 40.4 us -> 8.83 us
  Pallas kernels: 132 us -> 125 us
    unnamed x5 -> x0, local copies, waits for them, and re-layouts: 21.1 us -> none
    reshape x1 -> x0, local copies, waits for them, and re-layouts: 11.5 us -> none  [shards(): weights = base_key_value.reshape(features, nn, cols).transpose(1, 0, 2)]
    pallas_call x1 -> x0, Pallas kernels: 7.6 us -> none  [shards(): pl.pallas_call(pick, grid_spec=pltpu.PrefetchScalarGridSpec(num_scalar_pr...]
  transfers between devices with their start and end apart: 1 -> 1, of which waited for: 0 -> 1; matrix products, arithmetic and copies ran while one was open for 19% -> 3% of each run, Pallas kernels for 0% -> 0%
where the time goes in v2:
time: 145 us
  Pallas kernels  125 us (86%)
  local copies, waits for them, and re-layouts  8.83 us (6%)
  starting transfers between devices  6.28 us (4%)
  other arithmetic  4.54 us (3%)
    pallas_call x1, Pallas kernels, shards(): pl.pallas_call(functools.partial(main, nw, nx), out_shape=jax.ShapeDtypeS...  125 us
    all_to_all x1, starting transfers between devices, shards(): lax.all_to_all(wanted, 'wide', split_axis=0, concat_axis=0, tiled=True)  6.28 us
    transpose x1, local copies, waits for them, and re-layouts, shards(): return out.transpose(0, 2, 1, 3)  5.99 us
  transfers between devices with their start and end apart: 1, of which 1 were waited for; matrix products, arithmetic and copies ran while one was open for 3% of the time, Pallas kernels for 0%

profile of v2, /device:TPU:8, one launch (start us, length us, event | category | flops | bytes accessed | tf_op | source)
XLA Modules:
  0.0 145.1 jit_solution(12424808668260859806)
XLA Ops:
  0.0 1.2 broadcast_xor_fusion
  1.2 0.1 select_reduce_fusion
  1.3 0.7 copy.12
  2.0 6.3 %all-to-all-start = ((s32[8,1,1]{2,1,0:T(1,128)}), s32[8,1,1]{2,1,0:T(1,128)S(1)}, u32[]{:S(2)}, u32[]{:S(2)}) async-start(s32[8,1,1]{2,1,0:T(1,128)} %copy.12), calls=%async_computation | async-start | bytes 8192 | tf_op jit(solution)/shard_map/all_to_all | solution.py:218
  8.3 0.7 multiply_convert_fusion
  9.0 0.1 pad_maximum_fusion
  9.1 0.9 fusion
  10.0 0.7 multiply_sine_fusion
  10.7 2.2 %reshape.17.up = bf16[8,128,256]{2,1,0:T(8,128)(2,1)} reshape(bf16[8,2,64,2,128]{4,3,2,1,0:T(2,128)(2,1)} %param.9) | data formatting | bytes 1048576 | tf_op jit(solution)/shard_map/reshape | solution.py:222
  12.9 0.4 all-to-all-done
  13.3 0.8 maximum_reduce_fusion.chosen_ref
  14.1 125.0 %shard_map.64 = bf16[2,2,2048,128]{3,2,1,0:T(8,128)(2,1)} custom-call(s32[16]{0:T(128)} %get-tuple-element.5.slot_ref, s32[8]{0:T(128)} %maximum_reduce_fusion.chosen_ref, bf16[2048,2048]{1,0:T(8,128)(2,1)} %hid_hbm.1, bf16[2048,8,2,128]{3,2,1,0:T(2,128)(2,1)} %w_hbm.1, bf16[8,2048,128]{2,1,0:T(8,128)(2,1)} %store_hbm.1, bf16[8,128,256]{2,1,0:T(8,128)(2,1)} %reshape.17.up, ...), custom_call_target="tpu_custom_call" | custom-call | flops 25769803776 | bytes 33554432 | tf_op jit(solution)/shard_map/pallas_call | solution.py:233
  139.1 6.0 %copy.13 = bf16[2,2048,2,128]{3,2,1,0:T(2,128)(2,1)} copy(bf16[2,2048,2,128]{3,1,2,0:T(8,128)(2,1)} %bitcast.2) | data formatting | bytes 4194304 | tf_op jit(solution)/shard_map/transpose | solution.py:269
  (1 shorter events, 0.0 us)
Async XLA Ops:
  2.0 11.3 %all-to-all-start = ((s32[8,1,1]{2,1,0:T(1,128)}), s32[8,1,1]{2,1,0:T(1,128)S(1)}, u32[]{:S(2)}, u32[]{:S(2)}) async-start(s32[8,1,1]{2,1,0:T(1,128)} %copy.12), calls=%async_computation | async-start | bytes 8192 | tf_op jit(solution)/shard_map/all_to_all | solution.py:218
